TPU v7x, 32 devices: a whole 2x2x4 slice. The times are simulated.
32 devices in a mesh: sh: 4 (over z), sw: 4 (over y, core), tp: 2 (over x).
Axes of the slice: x: 2, y: 2, z: 4, core: 2. Of those that a mesh axis runs over, the one named last changes fastest.
Arguments:
- queries: bfloat16 [2, 32, 32, 1536], P('tp', 'sh', 'sw'), may hold values from -6 to 6
- keys: bfloat16 [2, 32, 32, 1536], P('tp', 'sh', 'sw'), may hold values from -6 to 6
- values: bfloat16 [2, 32, 32, 1536], P('tp', 'sh', 'sw'), may hold values from -6 to 6
- attn_out: bfloat16 [2, 32, 32, 1536], P('tp', 'sh', 'sw'), may hold values from -6 to 6
- attn_grad: bfloat16 [2, 32, 32, 1536], P('tp', 'sh', 'sw'), may hold values from -192 to 192
- log_sum: float32 [2, 32, 32, 12], P('tp', 'sh', 'sw'), may hold values from 6.1 to 6.9
- window_dirs: int32 [12, 4], replicated, may hold values from 0 to 7, as said below
Outputs:
- q_grad: bfloat16 [2, 32, 32, 1536], P('tp', 'sh', 'sw')
- k_grad: bfloat16 [2, 32, 32, 1536], P('tp', 'sh', 'sw')
- v_grad: bfloat16 [2, 32, 32, 1536], P('tp', 'sh', 'sw')
Inputs may be any that keep to these rules, and one draw needn't show every extreme that they name: `window_dirs`: each row names 4 different directions. Within each run of 6 consecutive heads (those of one index of tp) every direction is named by exactly half of the rows.
All inputs are finite; a program needn't handle non-finite values.
Results may differ from a plain program's by a relative error of at most 0.0056.
Values may be sent and summed in bfloat16 or wider, within the bound.
A program may use at most 64 MiB of HBM per device.

v0:
```python
import jax
import jax.numpy as jnp
from jax import lax
from jax.sharding import PartitionSpec as P

NEIGHBOURS = ((-1, -1), (-1, 0), (-1, 1), (0, -1), (0, 1), (1, -1), (1, 0), (1, 1))


def passed_along(block, axis, distance):
    devices = range(lax.axis_size(axis))
    route = [(i - distance, i) for i in devices if i - distance in devices]
    return lax.ppermute(block, axis, route)


def slot_tables(local_dirs):
    head_count = local_dirs.shape[0]
    half_heads = head_count // 2
    directions = jnp.arange(8, dtype=jnp.int32)
    listed = (local_dirs[:, :, None] == directions[None, None, :]).astype(jnp.int32)
    member = jnp.sum(listed, axis=1)
    position = jnp.sum(listed * jnp.arange(4, dtype=jnp.int32)[None, :, None], axis=1)
    rank_in = jnp.cumsum(member, axis=0) - 1
    slot_of = jnp.sum(listed * rank_in[:, None, :], axis=2)
    chosen = member[:, :, None] * (
        rank_in[:, :, None] == jnp.arange(half_heads, dtype=jnp.int32)[None, None, :]
    ).astype(jnp.int32)
    head_ids = jnp.arange(head_count, dtype=jnp.int32)
    head_of = jnp.sum(chosen * head_ids[:, None, None], axis=0)
    place_of = jnp.sum(chosen * position[:, :, None], axis=0)
    return (slot_of, head_of, place_of)


def bounds(offsets, direction_sign):
    grid_row = lax.axis_index("sh")
    grid_col = lax.axis_index("sw")
    target_row = grid_row + direction_sign * offsets[:, 0]
    target_col = grid_col + direction_sign * offsets[:, 1]
    inside = (
        (target_row >= 0)
        & (target_row < lax.axis_size("sh"))
        & (target_col >= 0)
        & (target_col < lax.axis_size("sw"))
    )
    return inside.astype(jnp.float32)


def pull_blocks(packs):
    arrived = {}
    for step_row in (-1, 1):
        stacked = jnp.stack(
            [packs[NEIGHBOURS.index((step_row, step_col))] for step_col in (-1, 0, 1)]
        )
        arrived[step_row] = passed_along(stacked, "sh", -step_row)
    result = {}
    for step_row in (-1, 1):
        result[step_row, 0] = arrived[step_row][1]
    for step_col in (-1, 1):
        column_pick = 0 if step_col < 0 else 2
        stacked = jnp.stack(
            [
                arrived[-1][column_pick],
                packs[NEIGHBOURS.index((0, step_col))],
                arrived[1][column_pick],
            ]
        )
        shifted = passed_along(stacked, "sw", -step_col)
        result[-1, step_col] = shifted[0]
        result[0, step_col] = shifted[1]
        result[1, step_col] = shifted[2]
    return jnp.stack([result[offset_pair] for offset_pair in NEIGHBOURS])


def send_out(packs, along_cols, along_rows):
    arrived = {}
    for step_col in (-1, 1):
        stacked = jnp.stack(
            [packs[NEIGHBOURS.index((step_row, step_col))] for step_row in (-1, 0, 1)]
        )
        arrived[step_col] = along_cols(stacked, step_col)
    result = {}
    for step_col in (-1, 1):
        result[0, step_col] = arrived[step_col][1]
    for step_row in (-1, 1):
        row_pick = 0 if step_row < 0 else 2
        stacked = jnp.stack(
            [arrived[-1][row_pick], packs[NEIGHBOURS.index((step_row, 0))], arrived[1][row_pick]]
        )
        shifted = along_rows(stacked, step_row)
        result[step_row, -1] = shifted[0]
        result[step_row, 0] = shifted[1]
        result[step_row, 1] = shifted[2]
    return jnp.stack([result[offset_pair] for offset_pair in NEIGHBOURS])


def local(queries, keys, values, attn_out, attn_grad, log_sum, window_dirs):
    frames_here, tile_rows, tile_cols, width_all = queries.shape
    head_total = log_sum.shape[3]
    head_dim = width_all // head_total
    row_delta = jnp.sum(
        (attn_grad.astype(jnp.float32) * attn_out.astype(jnp.float32)).reshape(
            frames_here, tile_rows, tile_cols, head_total, head_dim
        ),
        axis=4,
    )
    q_heads, k_heads, v_heads, g_heads = (
        lax.all_to_all(queries, "tp", split_axis=3, concat_axis=0, tiled=True),
        lax.all_to_all(keys, "tp", split_axis=3, concat_axis=0, tiled=True),
        lax.all_to_all(values, "tp", split_axis=3, concat_axis=0, tiled=True),
        lax.all_to_all(attn_grad, "tp", split_axis=3, concat_axis=0, tiled=True),
    )
    lse_heads, delta_heads = (
        lax.all_to_all(log_sum, "tp", split_axis=3, concat_axis=0, tiled=True),
        lax.all_to_all(row_delta, "tp", split_axis=3, concat_axis=0, tiled=True),
    )
    frames_all = q_heads.shape[0]
    head_here = q_heads.shape[3] // head_dim
    tile_tok = frames_all * tile_rows * tile_cols
    score_scale = head_dim ** (-0.5)

    def by_head(array):
        return jnp.transpose(array.reshape(tile_tok, head_here, head_dim), (1, 0, 2))

    q_own = by_head(q_heads)
    k_own = by_head(k_heads)
    v_own = by_head(v_heads)
    g_own = by_head(g_heads)
    lse_own = lse_heads.reshape(tile_tok, head_here).T
    delta_own = delta_heads.reshape(tile_tok, head_here).T
    local_dirs = lax.dynamic_slice_in_dim(
        window_dirs, lax.axis_index("tp") * head_here, head_here, 0
    )
    slot_of, head_of, place_of = slot_tables(local_dirs)
    offsets = jnp.array(NEIGHBOURS, dtype=jnp.int32)
    ahead_live = bounds(offsets, 1)
    kv_own = jnp.stack([k_own, v_own], axis=1)
    kv_packs = [jnp.take(kv_own, head_of[direction], axis=0) for direction in range(8)]
    recv_kv = pull_blocks(kv_packs)
    nb_kv = recv_kv[local_dirs, slot_of]
    k_all = jnp.concatenate([k_own[:, None], nb_kv[:, :, 0]], axis=1).reshape(
        head_here, 5 * tile_tok, head_dim
    )
    v_all = jnp.concatenate([v_own[:, None], nb_kv[:, :, 1]], axis=1).reshape(
        head_here, 5 * tile_tok, head_dim
    )
    live_all = jnp.concatenate(
        [
            jnp.ones((head_here, tile_tok), jnp.float32),
            jnp.repeat(ahead_live[local_dirs], tile_tok, axis=1),
        ],
        axis=1,
    )
    key_count = 5 * tile_tok
    contract_rows = (((0,), (0,)), ((), ()))
    contract_cols = (((1,), (1,)), ((), ()))

    def query_side(inputs):
        q_rows, g_rows, lse_row, delta_row, k_rows, v_rows, live_row = inputs
        scores = (
            lax.dot_general(q_rows, k_rows, contract_cols, preferred_element_type=jnp.float32)
            * score_scale
        )
        attn_prob = jnp.exp(scores - lse_row[:, None]) * live_row[None, :]
        grad_prob = lax.dot_general(
            g_rows, v_rows, contract_cols, preferred_element_type=jnp.float32
        )
        grad_score = attn_prob * (grad_prob - delta_row[:, None])
        score_bf = grad_score.astype(jnp.bfloat16)
        prob_bf = attn_prob.astype(jnp.bfloat16)
        q_grad = jnp.dot(score_bf, k_rows, preferred_element_type=jnp.float32) * score_scale
        k_part = (
            lax.dot_general(score_bf, q_rows, contract_rows, preferred_element_type=jnp.float32)
            * score_scale
        )
        v_part = lax.dot_general(prob_bf, g_rows, contract_rows, preferred_element_type=jnp.float32)
        return (q_grad, k_part, v_part)

    q_grad, k_part, v_part = lax.map(
        query_side, (q_own, g_own, lse_own, delta_own, k_all, v_all, live_all)
    )
    k_self = k_part[:, :tile_tok]
    v_self = v_part[:, :tile_tok]
    part_bf = jnp.stack(
        [
            k_part[:, tile_tok:].reshape(head_here, 4, tile_tok, head_dim),
            v_part[:, tile_tok:].reshape(head_here, 4, tile_tok, head_dim),
        ],
        axis=2,
    ).astype(jnp.bfloat16)
    part_packs = [part_bf[head_of[direction], place_of[direction]] for direction in range(8)]
    returned = send_out(
        part_packs,
        lambda moving, offset_step: passed_along(moving, "sw", offset_step),
        lambda moving, offset_step: passed_along(moving, "sh", offset_step),
    )
    mine_parts = returned[local_dirs, slot_of]
    summed = jnp.sum(mine_parts.astype(jnp.float32), axis=1)
    k_total = k_self + summed[:, 0]
    v_total = v_self + summed[:, 1]

    def by_token(array):
        return jnp.transpose(array.astype(jnp.bfloat16), (1, 0, 2)).reshape(
            frames_all, tile_rows, tile_cols, head_here * head_dim
        )

    return (
        lax.all_to_all(by_token(q_grad), "tp", split_axis=0, concat_axis=3, tiled=True),
        lax.all_to_all(by_token(k_total), "tp", split_axis=0, concat_axis=3, tiled=True),
        lax.all_to_all(by_token(v_total), "tp", split_axis=0, concat_axis=3, tiled=True),
    )


def solution(mesh):
    return jax.shard_map(
        local,
        mesh=mesh,
        in_specs=(
            P("tp", "sh", "sw", None),
            P("tp", "sh", "sw", None),
            P("tp", "sh", "sw", None),
            P("tp", "sh", "sw", None),
            P("tp", "sh", "sw", None),
            P("tp", "sh", "sw", None),
            P(),
        ),
        out_specs=(P("tp", "sh", "sw", None), P("tp", "sh", "sw", None), P("tp", "sh", "sw", None)),
        check_vma=False,
    )
```

profile of v0, /device:TPU:4, one launch (start us, length us, event | category | flops | bytes accessed | tf_op | source)
XLA Modules:
  0.0 248.6 jit_solution(4305474917567733513)
XLA Ops:
  0.6 3.2 %copy.106 = bf16[1,8,8,1536]{2,1,0,3:T(8,128)(2,1)S(1)} copy(bf16[1,8,8,1536]{3,2,1,0:T(8,128)(2,1)} %param.13) | data formatting | bytes 393216 | tf_op args[1]
  3.8 4.1 %reshape.753 = bf16[2,2,24576]{2,1,0:T(2,128)(2,1)} reshape(bf16[1536,1,8,8]{3,2,1,0:T(8,128)(2,1)S(1)} %bitcast.299) | data formatting | bytes 393216
  7.9 3.4 %all-to-all-start.1 = ((bf16[2,2,24576]{2,1,0:T(2,128)(2,1)}), bf16[2,2,24576]{2,1,0:T(2,128)(2,1)S(1)}, u32[]{:S(2)}, u32[]{:S(2)}) async-start(bf16[2,2,24576]{2,1,0:T(2,128)(2,1)} %reshape.753), calls=%async_computation.1 | async-start | bytes 393216 | tf_op jit(solution)/shard_map/all_to_all | solution.py:107
  24.6 2.2 copy.110
  26.8 4.1 %reshape.751 = bf16[2,2,24576]{2,1,0:T(2,128)(2,1)} reshape(bf16[1536,1,8,8]{3,2,1,0:T(8,128)(2,1)S(1)} %bitcast.300) | data formatting | bytes 393216
  30.9 4.1 %all-to-all-start.2 = ((bf16[2,2,24576]{2,1,0:T(2,128)(2,1)}), bf16[2,2,24576]{2,1,0:T(2,128)(2,1)}, u32[]{:S(2)}, u32[]{:S(2)}) async-start(bf16[2,2,24576]{2,1,0:T(2,128)(2,1)} %reshape.751), calls=%async_computation.2 | async-start | bytes 393216 | tf_op jit(solution)/shard_map/all_to_all | solution.py:108
  35.1 3.7 %reshape.754 = bf16[1536,1,8,8]{3,2,1,0:T(8,128)(2,1)S(1)} reshape(bf16[2,2,24576]{2,1,0:T(2,128)(2,1)S(1)} %all-to-all-done.1) | data formatting | bytes 393216
  38.7 2.4 copy.107
  42.3 3.3 %all-to-all-start.3 = ((f32[2,1,384]{2,1,0:T(1,128)}), f32[2,1,384]{2,1,0:T(1,128)S(1)}, u32[]{:S(2)}, u32[]{:S(2)}) async-start(f32[2,1,384]{2,1,0:T(1,128)} %reshape.755), calls=%async_computation.3 | async-start | bytes 6144 | tf_op jit(solution)/shard_map/all_to_all | solution.py:112
  45.6 4.5 %reshape.752 = bf16[1536,1,8,8]{3,2,1,0:T(8,128)(2,1)S(1)} reshape(bf16[2,2,24576]{2,1,0:T(2,128)(2,1)} %all-to-all-done.2) | data formatting | bytes 393216
  50.1 2.4 copy.111
  58.3 3.6 %collective-permute-start = (bf16[3,3,2,128,128]{4,3,2,1,0:T(8,128)(2,1)S(1)}, bf16[3,3,2,128,128]{4,3,2,1,0:T(8,128)(2,1)S(1)}, u32[]{:S(2)}, u32[]{:S(2)}) collective-permute-start(bf16[3,3,2,128,128]{4,3,2,1,0:T(8,128)(2,1)S(1)} %pad_maximum_fusion.4), channel_id=1, source_target_pairs={{0,8},{8,16},{16,24},{1,9},{9,17},{17,25},{2,10},{10,18},{18,26},{... | collective-permute-start | bytes 1769480 | tf_op jit(solution)/shard_map/ppermute | solution.py:12
  65.1 9.3 %collective-permute-done = bf16[3,3,2,128,128]{4,3,2,1,0:T(8,128)(2,1)S(1)} collective-permute-done((bf16[3,3,2,128,128]{4,3,2,1,0:T(8,128)(2,1)S(1)}, bf16[3,3,2,128,128]{4,3,2,1,0:T(8,128)(2,1)S(1)}, u32[]{:S(2)}, u32[]{:S(2)}) %collective-permute-start) | collective-permute-done | bytes 589856 | tf_op jit(solution)/shard_map/ppermute | solution.py:12
  74.4 4.5 %collective-permute-done.1 = bf16[3,3,2,128,128]{4,3,2,1,0:T(8,128)(2,1)S(1)} collective-permute-done((bf16[3,3,2,128,128]{4,3,2,1,0:T(8,128)(2,1)S(1)}, bf16[3,3,2,128,128]{4,3,2,1,0:T(8,128)(2,1)S(1)}, u32[]{:S(2)}, u32[]{:S(2)}) %collective-permute-start.1) | collective-permute-done | bytes 589856 | tf_op jit(solution)/shard_map/ppermute | solution.py:12
  79.0 1.9 collective-permute-start.2
  83.3 7.0 %collective-permute-done.2 = bf16[3,3,2,128,128]{4,3,2,1,0:T(8,128)(2,1)S(1)} collective-permute-done((bf16[3,3,2,128,128]{4,3,2,1,0:T(8,128)(2,1)S(1)}, bf16[3,3,2,128,128]{4,3,2,1,0:T(8,128)(2,1)S(1)}, u32[]{:S(2)}, u32[]{:S(2)}) %collective-permute-start.2) | collective-permute-done | bytes 589856 | tf_op jit(solution)/shard_map/ppermute | solution.py:12
  92.5 1.9 collective-permute-start.3
  94.5 3.4 %all-to-all-start.5 = ((f32[2,1,384]{2,1,0:T(1,128)}), f32[2,1,384]{2,1,0:T(1,128)S(1)}, u32[]{:S(2)}, u32[]{:S(2)}) async-start(f32[2,1,384]{2,1,0:T(1,128)} %reshape.759), calls=%async_computation.5 | async-start | bytes 6144 | tf_op jit(solution)/shard_map/all_to_all | solution.py:113
  98.4 3.1 %copy.104 = bf16[1,8,8,1536]{2,1,0,3:T(8,128)(2,1)S(1)} copy(bf16[1,8,8,1536]{3,2,1,0:T(8,128)(2,1)} %param.12) | data formatting | bytes 393216 | tf_op args[0]
  101.6 4.2 %reshape.749 = bf16[2,2,24576]{2,1,0:T(2,128)(2,1)} reshape(bf16[1536,1,8,8]{3,2,1,0:T(8,128)(2,1)S(1)} %bitcast.301) | data formatting | bytes 393216
  105.8 4.1 %all-to-all-start = ((bf16[2,2,24576]{2,1,0:T(2,128)(2,1)}), bf16[2,2,24576]{2,1,0:T(2,128)(2,1)}, u32[]{:S(2)}, u32[]{:S(2)}) async-start(bf16[2,2,24576]{2,1,0:T(2,128)(2,1)} %reshape.749), calls=%async_computation | async-start | bytes 393216 | tf_op jit(solution)/shard_map/all_to_all | solution.py:106
  111.2 3.1 %copy.118 = bf16[1,8,8,1536]{2,1,0,3:T(8,128)(2,1)S(1)} copy(bf16[1,8,8,1536]{3,2,1,0:T(8,128)(2,1)} %param.16) | data formatting | bytes 393216 | tf_op args[4]
  114.3 4.2 %reshape.757 = bf16[2,2,24576]{2,1,0:T(2,128)(2,1)} reshape(bf16[1536,1,8,8]{3,2,1,0:T(8,128)(2,1)S(1)} %bitcast.302) | data formatting | bytes 393216
  118.6 4.1 %all-to-all-start.4 = ((bf16[2,2,24576]{2,1,0:T(2,128)(2,1)}), bf16[2,2,24576]{2,1,0:T(2,128)(2,1)}, u32[]{:S(2)}, u32[]{:S(2)}) async-start(bf16[2,2,24576]{2,1,0:T(2,128)(2,1)} %reshape.757), calls=%async_computation.4 | async-start | bytes 393216 | tf_op jit(solution)/shard_map/all_to_all | solution.py:109
  128.3 4.5 %reshape.750 = bf16[1536,1,8,8]{3,2,1,0:T(8,128)(2,1)S(1)} reshape(bf16[2,2,24576]{2,1,0:T(2,128)(2,1)} %all-to-all-done) | data formatting | bytes 393216
  132.8 2.4 copy.105
  137.1 4.5 %reshape.758 = bf16[1536,1,8,8]{3,2,1,0:T(8,128)(2,1)S(1)} reshape(bf16[2,2,24576]{2,1,0:T(2,128)(2,1)} %all-to-all-done.4) | data formatting | bytes 393216
  141.6 2.4 copy.119
  150.1 1.6 slice_dynamic-update-slice_fusion.2
  151.7 1.6 slice_dynamic-update-slice_fusion.1
  154.9 2.3 gather_fusion
  158.3 29.2 %while.14 = (s32[]{:T(128)}, bf16[6,128,128]{2,1,0:T(8,128)(2,1)S(1)}, f32[6,640,128]{2,1,0:T(8,128)}, f32[6,640,128]{2,1,0:T(8,128)}, bf16[6,128,128]{2,1,0:T(8...) while((s32[]{:T(128)}, ...), condition=%wide.region_6.8_spmd, body=%wide.region_5.7_spmd.sunk | while | flops 105529344 | bytes 2835589 | solution.py:177
  161.4 1.7 fusion.131
  166.3 1.7 fusion.131
  171.1 1.7 fusion.131
  176.0 1.7 fusion.131
  180.9 1.7 fusion.131
  185.8 1.7 fusion.131
  193.0 1.9 collective-permute-start.4
  198.3 2.8 %collective-permute-start.5 = (bf16[3,3,2,128,128]{4,3,2,1,0:T(8,128)(2,1)}, bf16[3,3,2,128,128]{4,3,2,1,0:T(8,128)(2,1)}, u32[]{:S(2)}, u32[]{:S(2)}) collective-permute-start(bf16[3,3,2,128,128]{4,3,2,1,0:T(8,128)(2,1)} %pad_maximum_fusion.9), channel_id=1, source_target_pairs={{0,2},{2,4},{4,6},{1,3},{3,5},{5,7},{8,10},{10,12},{12,14},{9,11},... | collective-permute-start | bytes 1769480 | tf_op jit(solution)/shard_map/ppermute | solution.py:12
  203.7 6.1 %collective-permute-done.5 = bf16[3,3,2,128,128]{4,3,2,1,0:T(8,128)(2,1)} collective-permute-done((bf16[3,3,2,128,128]{4,3,2,1,0:T(8,128)(2,1)}, bf16[3,3,2,128,128]{4,3,2,1,0:T(8,128)(2,1)}, u32[]{:S(2)}, u32[]{:S(2)}) %collective-permute-start.5) | collective-permute-done | bytes 589856 | tf_op jit(solution)/shard_map/ppermute | solution.py:12
  211.0 3.5 %collective-permute-start.7 = (bf16[3,3,2,128,128]{4,3,2,1,0:T(8,128)(2,1)S(1)}, bf16[3,3,2,128,128]{4,3,2,1,0:T(8,128)(2,1)S(1)}, u32[]{:S(2)}, u32[]{:S(2)}) collective-permute-start(bf16[3,3,2,128,128]{4,3,2,1,0:T(8,128)(2,1)S(1)} %pad_maximum_fusion.11), channel_id=1, source_target_pairs={{0,8},{8,16},{16,24},{1,9},{9,17},{17,25},{2,10},{10,18},{18,26},{... | collective-permute-start | bytes 1769480 | tf_op jit(solution)/shard_map/ppermute | solution.py:12
  217.0 3.4 %all-to-all-start.6 = ((bf16[2,8,8,768]{3,2,1,0:T(8,128)(2,1)}), bf16[2,8,8,768]{3,2,1,0:T(8,128)(2,1)S(1)}, u32[]{:S(2)}, u32[]{:S(2)}) async-start(bf16[2,8,8,768]{3,2,1,0:T(8,128)(2,1)} %reshape.555), calls=%async_computation.6 | async-start | bytes 393216 | tf_op jit(solution)/shard_map/all_to_all | solution.py:206
  221.9 4.6 %collective-permute-done.6 = bf16[3,3,2,128,128]{4,3,2,1,0:T(8,128)(2,1)} collective-permute-done((bf16[3,3,2,128,128]{4,3,2,1,0:T(8,128)(2,1)S(1)}, bf16[3,3,2,128,128]{4,3,2,1,0:T(8,128)(2,1)}, u32[]{:S(2)}, u32[]{:S(2)}) %collective-permute-start.6) | collective-permute-done | bytes 589856 | tf_op jit(solution)/shard_map/ppermute | solution.py:12
  231.4 3.4 %all-to-all-start.8 = ((bf16[2,8,8,768]{3,2,1,0:T(8,128)(2,1)}), bf16[2,8,8,768]{3,2,1,0:T(8,128)(2,1)S(1)}, u32[]{:S(2)}, u32[]{:S(2)}) async-start(bf16[2,8,8,768]{3,2,1,0:T(8,128)(2,1)} %reshape.557), calls=%async_computation.8 | async-start | bytes 393216 | tf_op jit(solution)/shard_map/all_to_all | solution.py:208
  235.9 3.7 %all-to-all-done.8 = bf16[2,8,8,768]{3,2,1,0:T(8,128)(2,1)S(1)} async-done(((bf16[2,8,8,768]{3,2,1,0:T(8,128)(2,1)}), bf16[2,8,8,768]{3,2,1,0:T(8,128)(2,1)S(1)}, u32[]{:S(2)}, u32[]{:S(2)}) %all-to-all-start.8) | async-done | bytes 196640 | tf_op jit(solution)/shard_map/all_to_all | solution.py:208
  239.7 3.4 %all-to-all-start.7 = ((bf16[2,8,8,768]{3,2,1,0:T(8,128)(2,1)}), bf16[2,8,8,768]{3,2,1,0:T(8,128)(2,1)S(1)}, u32[]{:S(2)}, u32[]{:S(2)}) async-start(bf16[2,8,8,768]{3,2,1,0:T(8,128)(2,1)} %reshape.556), calls=%async_computation.7 | async-start | bytes 393216 | tf_op jit(solution)/shard_map/all_to_all | solution.py:207
  244.5 3.4 %all-to-all-done.7 = bf16[2,8,8,768]{3,2,1,0:T(8,128)(2,1)S(1)} async-done(((bf16[2,8,8,768]{3,2,1,0:T(8,128)(2,1)}), bf16[2,8,8,768]{3,2,1,0:T(8,128)(2,1)S(1)}, u32[]{:S(2)}, u32[]{:S(2)}) %all-to-all-start.7) | async-done | bytes 196640 | tf_op jit(solution)/shard_map/all_to_all | solution.py:207
  (263 shorter events, 88.9 us)
Async XLA Ops:
  3.8 7.5 %copy-start.16 = (s32[12,4]{0,1:T(4,128)S(1)}, s32[12,4]{0,1:T(4,128)}, u32[]{:S(2)}) copy-start(s32[12,4]{0,1:T(4,128)} %param.18) | copy-start | bytes 580
  3.8 20.8 %copy-start.4 = (bf16[1,8,8,1536]{3,2,1,0:T(8,128)(2,1)S(1)}, bf16[1,8,8,1536]{3,2,1,0:T(8,128)(2,1)}, u32[]{:S(2)}) copy-start(bf16[1,8,8,1536]{3,2,1,0:T(8,128)(2,1)} %param.14) | copy-start | bytes 589828
  7.9 23.1 %all-to-all-start.1 = ((bf16[2,2,24576]{2,1,0:T(2,128)(2,1)}), bf16[2,2,24576]{2,1,0:T(2,128)(2,1)S(1)}, u32[]{:S(2)}, u32[]{:S(2)}) async-start(bf16[2,2,24576]{2,1,0:T(2,128)(2,1)} %reshape.753), calls=%async_computation.1 | async-start | bytes 393216 | tf_op jit(solution)/shard_map/all_to_all | solution.py:107
  12.8 9.5 %copy-start.17 = (s32[3]{0:T(128)}, s32[3]{0:T(128)S(1)}, u32[]{:S(2)}) copy-start(s32[3]{0:T(128)S(1)} %get-tuple-element.188) | copy-start | bytes 40
  12.8 9.5 %copy-start.18 = (s32[3]{0:T(128)}, s32[3]{0:T(128)S(1)}, u32[]{:S(2)}) copy-start(s32[3]{0:T(128)S(1)} %get-tuple-element.184) | copy-start | bytes 40
  12.8 9.5 %copy-start.19 = (s32[3]{0:T(128)}, s32[3]{0:T(128)S(1)}, u32[]{:S(2)}) copy-start(s32[3]{0:T(128)S(1)} %get-tuple-element.185) | copy-start | bytes 40
  12.8 9.5 %copy-start.20 = (s32[3]{0:T(128)}, s32[3]{0:T(128)S(1)}, u32[]{:S(2)}) copy-start(s32[3]{0:T(128)S(1)} %get-tuple-element.183) | copy-start | bytes 40
  12.8 9.5 %copy-start.21 = (s32[3]{0:T(128)}, s32[3]{0:T(128)S(1)}, u32[]{:S(2)}) copy-start(s32[3]{0:T(128)S(1)} %get-tuple-element.186) | copy-start | bytes 40
  12.8 9.6 %copy-start.23 = (s32[3]{0:T(128)}, s32[3]{0:T(128)S(1)}, u32[]{:S(2)}) copy-start(s32[3]{0:T(128)S(1)} %get-tuple-element.187) | copy-start | bytes 40
  26.8 4.1 %copy-start.34 = (s32[8,1]{0,1:T(1,128)S(1)}, s32[8,1]{0,1:T(1,128)}, u32[]{:S(2)}) copy-start(s32[8,1]{0,1:T(1,128)} %constant.90) | copy-start | bytes 100
  26.8 4.1 %copy-start.35 = (s32[8,1]{0,1:T(1,128)S(1)}, s32[8,1]{0,1:T(1,128)}, u32[]{:S(2)}) copy-start(s32[8,1]{0,1:T(1,128)} %constant.89) | copy-start | bytes 100
  26.8 4.1 %copy-start.37 = (s32[3]{0:T(128)S(1)}, s32[3]{0:T(128)}, u32[]{:S(2)}) copy-start(s32[3]{0:T(128)} %compare_select_fusion.8) | copy-start | bytes 40
  26.8 8.2 %copy-start.36 = (s32[3]{0:T(128)S(1)}, s32[3]{0:T(128)}, u32[]{:S(2)}) copy-start(s32[3]{0:T(128)} %compare_select_fusion.9) | copy-start | bytes 40
  30.9 11.3 %all-to-all-start.2 = ((bf16[2,2,24576]{2,1,0:T(2,128)(2,1)}), bf16[2,2,24576]{2,1,0:T(2,128)(2,1)}, u32[]{:S(2)}, u32[]{:S(2)}) async-start(bf16[2,2,24576]{2,1,0:T(2,128)(2,1)} %reshape.751), calls=%async_computation.2 | async-start | bytes 393216 | tf_op jit(solution)/shard_map/all_to_all | solution.py:108
  42.3 52.1 %all-to-all-start.3 = ((f32[2,1,384]{2,1,0:T(1,128)}), f32[2,1,384]{2,1,0:T(1,128)S(1)}, u32[]{:S(2)}, u32[]{:S(2)}) async-start(f32[2,1,384]{2,1,0:T(1,128)} %reshape.755), calls=%async_computation.3 | async-start | bytes 6144 | tf_op jit(solution)/shard_map/all_to_all | solution.py:112
  53.7 4.1 %copy-start.32 = (pred[3]{0:T(512)(128)(4,1)S(1)}, pred[3]{0:T(512)(128)(4,1)}, u32[]{:S(2)}) copy-start(pred[3]{0:T(512)(128)(4,1)} %compare_and_fusion.5) | copy-start | bytes 13
  53.8 4.2 %copy-start.31 = (pred[3]{0:T(512)(128)(4,1)S(1)}, pred[3]{0:T(512)(128)(4,1)}, u32[]{:S(2)}) copy-start(pred[3]{0:T(512)(128)(4,1)} %compare_and_fusion.7) | copy-start | bytes 13
  53.8 4.3 %copy-start.30 = (pred[3]{0:T(512)(128)(4,1)S(1)}, pred[3]{0:T(512)(128)(4,1)}, u32[]{:S(2)}) copy-start(pred[3]{0:T(512)(128)(4,1)} %compare_and_fusion.6) | copy-start | bytes 13
  56.6 5.3 %copy-start.29 = (pred[3]{0:T(512)(128)(4,1)S(1)}, pred[3]{0:T(512)(128)(4,1)}, u32[]{:S(2)}) copy-start(pred[3]{0:T(512)(128)(4,1)} %compare_and_fusion.1) | copy-start | bytes 13
  57.2 4.8 %copy-start.28 = (pred[3]{0:T(512)(128)(4,1)S(1)}, pred[3]{0:T(512)(128)(4,1)}, u32[]{:S(2)}) copy-start(pred[3]{0:T(512)(128)(4,1)} %compare_and_fusion.2) | copy-start | bytes 13
  57.9 4.3 %copy-start.27 = (pred[3]{0:T(512)(128)(4,1)S(1)}, pred[3]{0:T(512)(128)(4,1)}, u32[]{:S(2)}) copy-start(pred[3]{0:T(512)(128)(4,1)} %compare_and_fusion.3) | copy-start | bytes 13
  58.2 5.5 %copy-start = (bf16[1,8,8,1536]{3,2,1,0:T(8,128)(2,1)S(1)}, bf16[1,8,8,1536]{3,2,1,0:T(8,128)(2,1)}, u32[]{:S(2)}) copy-start(bf16[1,8,8,1536]{3,2,1,0:T(8,128)(2,1)} %param.16) | copy-start | bytes 589828
  58.2 5.4 %copy-start.5 = (bf16[1,8,8,1536]{3,2,1,0:T(8,128)(2,1)S(1)}, bf16[1,8,8,1536]{3,2,1,0:T(8,128)(2,1)}, u32[]{:S(2)}) copy-start(bf16[1,8,8,1536]{3,2,1,0:T(8,128)(2,1)} %param.15) | copy-start | bytes 589828
  58.3 6.7 %copy-start.26 = (pred[3]{0:T(512)(128)(4,1)S(1)}, pred[3]{0:T(512)(128)(4,1)}, u32[]{:S(2)}) copy-start(pred[3]{0:T(512)(128)(4,1)} %compare_and_fusion.4) | copy-start | bytes 13
  58.3 16.1 %collective-permute-start = (bf16[3,3,2,128,128]{4,3,2,1,0:T(8,128)(2,1)S(1)}, bf16[3,3,2,128,128]{4,3,2,1,0:T(8,128)(2,1)S(1)}, u32[]{:S(2)}, u32[]{:S(2)}) collective-permute-start(bf16[3,3,2,128,128]{4,3,2,1,0:T(8,128)(2,1)S(1)} %pad_maximum_fusion.4), channel_id=1, source_target_pairs={{0,8},{8,16},{16,24},{1,9},{9,17},{17,25},{2,10},{10,18},{18,26},{... | collective-permute-start | bytes 1769480 | tf_op jit(solution)/shard_map/ppermute | solution.py:12
  62.3 16.6 %collective-permute-start.1 = (bf16[3,3,2,128,128]{4,3,2,1,0:T(8,128)(2,1)S(1)}, bf16[3,3,2,128,128]{4,3,2,1,0:T(8,128)(2,1)S(1)}, u32[]{:S(2)}, u32[]{:S(2)}) collective-permute-start(bf16[3,3,2,128,128]{4,3,2,1,0:T(8,128)(2,1)S(1)} %pad_maximum_fusion.5), channel_id=1, source_target_pairs={{8,0},{16,8},{24,16},{9,1},{17,9},{25,17},{10,2},{18,10},{26,18},{... | collective-permute-start | bytes 1769480 | tf_op jit(solution)/shard_map/ppermute | solution.py:12
  64.4 16.5 %copy-start.15 = (s32[24]{0:T(128)S(1)}, s32[24]{0:T(128)}, u32[]{:S(2)}) copy-start(s32[24]{0:T(128)} %reshape.632) | copy-start | bytes 292
  79.0 11.2 %collective-permute-start.2 = (bf16[3,3,2,128,128]{4,3,2,1,0:T(8,128)(2,1)S(1)}, bf16[3,3,2,128,128]{4,3,2,1,0:T(8,128)(2,1)S(1)}, u32[]{:S(2)}, u32[]{:S(2)}) collective-permute-start(bf16[3,3,2,128,128]{4,3,2,1,0:T(8,128)(2,1)S(1)} %pad_maximum_fusion.6), channel_id=1, source_target_pairs={{0,2},{2,4},{4,6},{1,3},{3,5},{5,7},{8,10},{10,12},{12,14},{9,11},... | collective-permute-start | bytes 1769480 | tf_op jit(solution)/shard_map/ppermute | solution.py:12
  82.6 15.3 %copy-start.22 = (s32[3]{0:T(128)S(1)}, s32[3]{0:T(128)}, u32[]{:S(2)}) copy-start(s32[3]{0:T(128)} %get-tuple-element.130) | copy-start | bytes 40
  82.6 15.3 %copy-start.24 = (s32[3]{0:T(128)S(1)}, s32[3]{0:T(128)}, u32[]{:S(2)}) copy-start(s32[3]{0:T(128)} %copy-done.23) | copy-start | bytes 40
  90.2 7.6 %copy-start.2 = (bf16[3,3,2,128,128]{4,3,2,1,0:T(8,128)(2,1)}, bf16[3,3,2,128,128]{4,3,2,1,0:T(8,128)(2,1)S(1)}, u32[]{:S(2)}) copy-start(bf16[3,3,2,128,128]{4,3,2,1,0:T(8,128)(2,1)S(1)} %collective-permute-done.2) | copy-start | bytes 1769476
  92.5 52.7 %collective-permute-start.3 = (bf16[3,3,2,128,128]{4,3,2,1,0:T(8,128)(2,1)}, bf16[3,3,2,128,128]{4,3,2,1,0:T(8,128)(2,1)}, u32[]{:S(2)}, u32[]{:S(2)}) collective-permute-start(bf16[3,3,2,128,128]{4,3,2,1,0:T(8,128)(2,1)} %pad_maximum_fusion.7), channel_id=1, source_target_pairs={{2,0},{4,2},{6,4},{3,1},{5,3},{7,5},{10,8},{12,10},{14,12},{11,9},... | collective-permute-start | bytes 1769480 | tf_op jit(solution)/shard_map/ppermute | solution.py:12
  94.4 3.4 %copy-start.7 = (f32[2,1,384]{2,1,0:T(1,128)}, f32[2,1,384]{2,1,0:T(1,128)S(1)}, u32[]{:S(2)}) copy-start(f32[2,1,384]{2,1,0:T(1,128)S(1)} %all-to-all-done.3) | copy-start | bytes 9220
  94.5 11.3 %all-to-all-start.5 = ((f32[2,1,384]{2,1,0:T(1,128)}), f32[2,1,384]{2,1,0:T(1,128)S(1)}, u32[]{:S(2)}, u32[]{:S(2)}) async-start(f32[2,1,384]{2,1,0:T(1,128)} %reshape.759), calls=%async_computation.5 | async-start | bytes 6144 | tf_op jit(solution)/shard_map/all_to_all | solution.py:113
  105.8 8.5 %copy-start.8 = (f32[2,1,384]{2,1,0:T(1,128)}, f32[2,1,384]{2,1,0:T(1,128)S(1)}, u32[]{:S(2)}) copy-start(f32[2,1,384]{2,1,0:T(1,128)S(1)} %all-to-all-done.5) | copy-start | bytes 9220
  105.8 12.8 %all-to-all-start = ((bf16[2,2,24576]{2,1,0:T(2,128)(2,1)}), bf16[2,2,24576]{2,1,0:T(2,128)(2,1)}, u32[]{:S(2)}, u32[]{:S(2)}) async-start(bf16[2,2,24576]{2,1,0:T(2,128)(2,1)} %reshape.749), calls=%async_computation | async-start | bytes 393216 | tf_op jit(solution)/shard_map/all_to_all | solution.py:106
  114.3 9.6 %copy-start.14 = (s32[6,4,1]{0,1,2:T(4,128)S(1)}, s32[6,4,1]{0,1,2:T(4,128)}, u32[]{:S(2)}) copy-start(s32[6,4,1]{0,1,2:T(4,128)} %fusion.43) | copy-start | bytes 292
  118.6 18.5 %all-to-all-start.4 = ((bf16[2,2,24576]{2,1,0:T(2,128)(2,1)}), bf16[2,2,24576]{2,1,0:T(2,128)(2,1)}, u32[]{:S(2)}, u32[]{:S(2)}) async-start(bf16[2,2,24576]{2,1,0:T(2,128)(2,1)} %reshape.757), calls=%async_computation.4 | async-start | bytes 393216 | tf_op jit(solution)/shard_map/all_to_all | solution.py:109
  191.1 4.5 %copy-start.9 = (s32[3]{0:T(128)S(1)}, s32[3]{0:T(128)}, u32[]{:S(2)}) copy-start(s32[3]{0:T(128)} %fusion.86) | copy-start | bytes 40
  191.1 5.1 %copy-start.10 = (s32[3]{0:T(128)S(1)}, s32[3]{0:T(128)}, u32[]{:S(2)}) copy-start(s32[3]{0:T(128)} %fusion.87) | copy-start | bytes 40
  193.0 10.7 %collective-permute-start.4 = (bf16[3,3,2,128,128]{4,3,2,1,0:T(8,128)(2,1)S(1)}, bf16[3,3,2,128,128]{4,3,2,1,0:T(8,128)(2,1)S(1)}, u32[]{:S(2)}, u32[]{:S(2)}) collective-permute-start(bf16[3,3,2,128,128]{4,3,2,1,0:T(8,128)(2,1)S(1)} %pad_maximum_fusion.8), channel_id=1, source_target_pairs={{2,0},{4,2},{6,4},{3,1},{5,3},{7,5},{10,8},{12,10},{14,12},{11,9},... | collective-permute-start | bytes 1769480 | tf_op jit(solution)/shard_map/ppermute | solution.py:12
  198.3 11.5 %collective-permute-start.5 = (bf16[3,3,2,128,128]{4,3,2,1,0:T(8,128)(2,1)}, bf16[3,3,2,128,128]{4,3,2,1,0:T(8,128)(2,1)}, u32[]{:S(2)}, u32[]{:S(2)}) collective-permute-start(bf16[3,3,2,128,128]{4,3,2,1,0:T(8,128)(2,1)} %pad_maximum_fusion.9), channel_id=1, source_target_pairs={{0,2},{2,4},{4,6},{1,3},{3,5},{5,7},{8,10},{10,12},{12,14},{9,11},... | collective-permute-start | bytes 1769480 | tf_op jit(solution)/shard_map/ppermute | solution.py:12
  211.0 10.8 %collective-permute-start.7 = (bf16[3,3,2,128,128]{4,3,2,1,0:T(8,128)(2,1)S(1)}, bf16[3,3,2,128,128]{4,3,2,1,0:T(8,128)(2,1)S(1)}, u32[]{:S(2)}, u32[]{:S(2)}) collective-permute-start(bf16[3,3,2,128,128]{4,3,2,1,0:T(8,128)(2,1)S(1)} %pad_maximum_fusion.11), channel_id=1, source_target_pairs={{0,8},{8,16},{16,24},{1,9},{9,17},{17,25},{2,10},{10,18},{18,26},{... | collective-permute-start | bytes 1769480 | tf_op jit(solution)/shard_map/ppermute | solution.py:12
  214.6 11.9 %collective-permute-start.6 = (bf16[3,3,2,128,128]{4,3,2,1,0:T(8,128)(2,1)S(1)}, bf16[3,3,2,128,128]{4,3,2,1,0:T(8,128)(2,1)}, u32[]{:S(2)}, u32[]{:S(2)}) collective-permute-start(bf16[3,3,2,128,128]{4,3,2,1,0:T(8,128)(2,1)S(1)} %pad_maximum_fusion.10), channel_id=1, source_target_pairs={{8,0},{16,8},{24,16},{9,1},{17,9},{25,17},{10,2},{18,10},{26,18},{... | collective-permute-start | bytes 1769480 | tf_op jit(solution)/shard_map/ppermute | solution.py:12
  217.0 14.4 %all-to-all-start.6 = ((bf16[2,8,8,768]{3,2,1,0:T(8,128)(2,1)}), bf16[2,8,8,768]{3,2,1,0:T(8,128)(2,1)S(1)}, u32[]{:S(2)}, u32[]{:S(2)}) async-start(bf16[2,8,8,768]{3,2,1,0:T(8,128)(2,1)} %reshape.555), calls=%async_computation.6 | async-start | bytes 393216 | tf_op jit(solution)/shard_map/all_to_all | solution.py:206
  221.9 4.6 %copy-start.3 = (bf16[3,3,2,128,128]{4,3,2,1,0:T(8,128)(2,1)}, bf16[3,3,2,128,128]{4,3,2,1,0:T(8,128)(2,1)S(1)}, u32[]{:S(2)}) copy-start(bf16[3,3,2,128,128]{4,3,2,1,0:T(8,128)(2,1)S(1)} %collective-permute-done.7) | copy-start | bytes 1769476
  231.4 8.2 %all-to-all-start.8 = ((bf16[2,8,8,768]{3,2,1,0:T(8,128)(2,1)}), bf16[2,8,8,768]{3,2,1,0:T(8,128)(2,1)S(1)}, u32[]{:S(2)}, u32[]{:S(2)}) async-start(bf16[2,8,8,768]{3,2,1,0:T(8,128)(2,1)} %reshape.557), calls=%async_computation.8 | async-start | bytes 393216 | tf_op jit(solution)/shard_map/all_to_all | solution.py:208
  239.7 8.2 %all-to-all-start.7 = ((bf16[2,8,8,768]{3,2,1,0:T(8,128)(2,1)}), bf16[2,8,8,768]{3,2,1,0:T(8,128)(2,1)S(1)}, u32[]{:S(2)}, u32[]{:S(2)}) async-start(bf16[2,8,8,768]{3,2,1,0:T(8,128)(2,1)} %reshape.556), calls=%async_computation.7 | async-start | bytes 393216 | tf_op jit(solution)/shard_map/all_to_all | solution.py:207
  (7 other events, 10.9 us)
where the time goes:
time: 252 us; the launch traced here: 249 us
  local copies, waits for them, and re-layouts  107 us (42%)
  starting transfers between devices  51 us (20%)
  waiting for transfers between devices  40.1 us (16%)
  matrix products  24.6 us (10%)
  other arithmetic  24.4 us (10%)
    unnamed x101, local copies, waits for them, and re-layouts  58.1 us
    ppermute x8, waiting for transfers between devices, passed_along(): return lax.ppermute(block, axis, route)  32.9 us
    ppermute x8, starting transfers between devices, passed_along(): return lax.ppermute(block, axis, route)  18.3 us
    dot_general x6, matrix products, query_side(): lax.dot_general(score_bf, q_rows, contract_rows, preferred_element_type=j...  10.3 us
    concatenate x8, other arithmetic, local(): part_bf[head_of[direction], place_of[direction]]  6.04 us
    dot_general x6, matrix products, query_side(): lax.dot_general(q_rows, k_rows, contract_cols, preferred_element_type=jnp...  5.93 us
    dot_general x6, matrix products, query_side(): lax.dot_general(prob_bf, g_rows, contract_rows, preferred_element_type=jn...  5.82 us
    gather x8, local copies, waits for them, and re-layouts, local(): jnp.take(kv_own, head_of[direction], axis=0)  5.17 us
  transfers between devices with their start and end apart: 17, of which 8 were waited for; matrix products, arithmetic and copies ran while one was open for 40% of the time, Pallas kernels for 0%

commit v1 on v0

--- a/solution.py
+++ b/solution.py
@@ -4,6 +4,18 @@
 from jax.sharding import PartitionSpec as P
 
 NEIGHBOURS = ((-1, -1), (-1, 0), (-1, 1), (0, -1), (0, 1), (1, -1), (1, 0), (1, 1))
+
+
+def _drive_keys(in_array):
+    return jnp.concatenate(
+        lax.all_to_all(
+            jnp.stack(jnp.split(in_array, lax.axis_size("tp"), 3), 0),
+            axis_name="tp",
+            split_axis=0,
+            concat_axis=0,
+        ),
+        0,
+    )
 
 
 def passed_along(block, axis, distance):
@@ -105,7 +117,7 @@
     q_heads, k_heads, v_heads, g_heads = (
         lax.all_to_all(queries, "tp", split_axis=3, concat_axis=0, tiled=True),
         lax.all_to_all(keys, "tp", split_axis=3, concat_axis=0, tiled=True),
-        lax.all_to_all(values, "tp", split_axis=3, concat_axis=0, tiled=True),
+        _drive_keys(values),
         lax.all_to_all(attn_grad, "tp", split_axis=3, concat_axis=0, tiled=True),
     )
     lse_heads, delta_heads = (

time: 252 us -> 242 us (0.960)
  local copies, waits for them, and re-layouts: 107 us -> 91.6 us
  other arithmetic: 24.4 us -> 27.8 us
  waiting for transfers between devices: 40.1 us -> 42.9 us
    unnamed x101 -> x94, local copies, waits for them, and re-layouts: 58.1 us -> 46.4 us
    all_to_all x1, waiting for transfers between devices: 0.01 us -> 3.92 us  [local(): lax.all_to_all(keys, 'tp', split_axis=3, concat_axis=0, tiled=True)]
  transfers between devices with their start and end apart: 17 -> 17, of which waited for: 8 -> 9; matrix products, arithmetic and copies ran while one was open for 40% -> 39% of each run, Pallas kernels for 0% -> 0%
where the time goes in v1:
time: 242 us; the launch traced here: 239 us
  local copies, waits for them, and re-layouts  91.6 us (38%)
  starting transfers between devices  50.6 us (21%)
  waiting for transfers between devices  42.9 us (18%)
  other arithmetic  27.8 us (11%)
  matrix products  24.6 us (10%)
    unnamed x94, local copies, waits for them, and re-layouts  46.4 us
    ppermute x8, waiting for transfers between devices, passed_along(): return lax.ppermute(block, axis, route)  31.8 us
    ppermute x8, starting transfers between devices, passed_along(): return lax.ppermute(block, axis, route)  18.1 us
    dot_general x6, matrix products, query_side(): lax.dot_general(score_bf, q_rows, contract_rows, preferred_element_type=j...  10.3 us
    concatenate x8, other arithmetic, local(): part_bf[head_of[direction], place_of[direction]]  6.04 us
    dot_general x6, matrix products, query_side(): lax.dot_general(q_rows, k_rows, contract_cols, preferred_element_type=jnp...  5.94 us
    dot_general x6, matrix products, query_side(): lax.dot_general(prob_bf, g_rows, contract_rows, preferred_element_type=jn...  5.82 us
    gather x8, local copies, waits for them, and re-layouts, local(): jnp.take(kv_own, head_of[direction], axis=0)  5.66 us
  transfers between devices with their start and end apart: 17, of which 9 were waited for; matrix products, arithmetic and copies ran while one was open for 39% of the time, Pallas kernels for 0%

profile of v1, /device:TPU:4, one launch (start us, length us, event | category | flops | bytes accessed | tf_op | source)
XLA Modules:
  0.0 239.3 jit_solution(3162273360823972988)
XLA Ops:
  2.3 3.4 %all-to-all-start.2 = ((bf16[2,1,8,8,768]{4,3,2,1,0:T(8,128)(2,1)}), bf16[2,1,8,8,768]{4,3,2,1,0:T(8,128)(2,1)S(1)}, u32[]{:S(2)}, u32[]{:S(2)}) async-start(bf16[2,1,8,8,768]{4,3,2,1,0:T(8,128)(2,1)} %pad_maximum_fusion.13), calls=%async_computation.2 | async-start | bytes 393216 | tf_op jit(solution)/shard_map/all_to_all | solution.py:11
  20.6 2.2 copy.101
  22.9 4.1 %reshape.746 = bf16[2,2,24576]{2,1,0:T(2,128)(2,1)} reshape(bf16[1536,1,8,8]{3,2,1,0:T(8,128)(2,1)S(1)} %bitcast.298) | data formatting | bytes 393216
  27.6 3.4 %all-to-all-start.1 = ((bf16[2,2,24576]{2,1,0:T(2,128)(2,1)}), bf16[2,2,24576]{2,1,0:T(2,128)(2,1)S(1)}, u32[]{:S(2)}, u32[]{:S(2)}) async-start(bf16[2,2,24576]{2,1,0:T(2,128)(2,1)} %reshape.746), calls=%async_computation.1 | async-start | bytes 393216 | tf_op jit(solution)/shard_map/all_to_all | solution.py:119
  31.9 3.9 %all-to-all-done.1 = bf16[2,2,24576]{2,1,0:T(2,128)(2,1)S(1)} async-done(((bf16[2,2,24576]{2,1,0:T(2,128)(2,1)}), bf16[2,2,24576]{2,1,0:T(2,128)(2,1)S(1)}, u32[]{:S(2)}, u32[]{:S(2)}) %all-to-all-start.1) | async-done | bytes 196640 | tf_op jit(solution)/shard_map/all_to_all | solution.py:119
  35.8 3.8 %all-to-all-start.3 = ((f32[2,1,384]{2,1,0:T(1,128)}), f32[2,1,384]{2,1,0:T(1,128)}, u32[]{:S(2)}, u32[]{:S(2)}) async-start(f32[2,1,384]{2,1,0:T(1,128)} %reshape.748), calls=%async_computation.3 | async-start | bytes 6144 | tf_op jit(solution)/shard_map/all_to_all | solution.py:124
  39.6 3.7 %reshape.747 = bf16[1536,1,8,8]{3,2,1,0:T(8,128)(2,1)S(1)} reshape(bf16[2,2,24576]{2,1,0:T(2,128)(2,1)S(1)} %all-to-all-done.1) | data formatting | bytes 393216
  43.3 1.6 copy.102
  50.0 3.6 %collective-permute-start = (bf16[3,3,2,128,128]{4,3,2,1,0:T(8,128)(2,1)S(1)}, bf16[3,3,2,128,128]{4,3,2,1,0:T(8,128)(2,1)S(1)}, u32[]{:S(2)}, u32[]{:S(2)}) collective-permute-start(bf16[3,3,2,128,128]{4,3,2,1,0:T(8,128)(2,1)S(1)} %pad_maximum_fusion.4), channel_id=1, source_target_pairs={{0,8},{8,16},{16,24},{1,9},{9,17},{17,25},{2,10},{10,18},{18,26},{... | collective-permute-start | bytes 1769480 | tf_op jit(solution)/shard_map/ppermute | solution.py:24
  57.1 8.0 %collective-permute-done = bf16[3,3,2,128,128]{4,3,2,1,0:T(8,128)(2,1)S(1)} collective-permute-done((bf16[3,3,2,128,128]{4,3,2,1,0:T(8,128)(2,1)S(1)}, bf16[3,3,2,128,128]{4,3,2,1,0:T(8,128)(2,1)S(1)}, u32[]{:S(2)}, u32[]{:S(2)}) %collective-permute-start) | collective-permute-done | bytes 589856 | tf_op jit(solution)/shard_map/ppermute | solution.py:24
  65.1 4.5 %collective-permute-done.1 = bf16[3,3,2,128,128]{4,3,2,1,0:T(8,128)(2,1)S(1)} collective-permute-done((bf16[3,3,2,128,128]{4,3,2,1,0:T(8,128)(2,1)S(1)}, bf16[3,3,2,128,128]{4,3,2,1,0:T(8,128)(2,1)S(1)}, u32[]{:S(2)}, u32[]{:S(2)}) %collective-permute-start.1) | collective-permute-done | bytes 589856 | tf_op jit(solution)/shard_map/ppermute | solution.py:24
  69.7 1.9 collective-permute-start.2
  73.9 7.0 %collective-permute-done.2 = bf16[3,3,2,128,128]{4,3,2,1,0:T(8,128)(2,1)S(1)} collective-permute-done((bf16[3,3,2,128,128]{4,3,2,1,0:T(8,128)(2,1)S(1)}, bf16[3,3,2,128,128]{4,3,2,1,0:T(8,128)(2,1)S(1)}, u32[]{:S(2)}, u32[]{:S(2)}) %collective-permute-start.2) | collective-permute-done | bytes 589856 | tf_op jit(solution)/shard_map/ppermute | solution.py:24
  83.2 1.9 collective-permute-start.3
  85.1 3.2 %all-to-all-start.5 = ((f32[2,1,384]{2,1,0:T(1,128)}), f32[2,1,384]{2,1,0:T(1,128)S(1)}, u32[]{:S(2)}, u32[]{:S(2)}) async-start(f32[2,1,384]{2,1,0:T(1,128)} %reshape.752), calls=%async_computation.5 | async-start | bytes 6144 | tf_op jit(solution)/shard_map/all_to_all | solution.py:125
  88.9 3.1 %copy.99 = bf16[1,8,8,1536]{2,1,0,3:T(8,128)(2,1)S(1)} copy(bf16[1,8,8,1536]{3,2,1,0:T(8,128)(2,1)} %param.12) | data formatting | bytes 393216 | tf_op args[0]
  92.0 4.2 %reshape.744 = bf16[2,2,24576]{2,1,0:T(2,128)(2,1)} reshape(bf16[1536,1,8,8]{3,2,1,0:T(8,128)(2,1)S(1)} %bitcast.299) | data formatting | bytes 393216
  96.3 4.3 %all-to-all-start = ((bf16[2,2,24576]{2,1,0:T(2,128)(2,1)}), bf16[2,2,24576]{2,1,0:T(2,128)(2,1)}, u32[]{:S(2)}, u32[]{:S(2)}) async-start(bf16[2,2,24576]{2,1,0:T(2,128)(2,1)} %reshape.744), calls=%async_computation | async-start | bytes 393216 | tf_op jit(solution)/shard_map/all_to_all | solution.py:118
  101.8 3.1 %copy.111 = bf16[1,8,8,1536]{2,1,0,3:T(8,128)(2,1)S(1)} copy(bf16[1,8,8,1536]{3,2,1,0:T(8,128)(2,1)} %param.16) | data formatting | bytes 393216 | tf_op args[4]
  105.0 4.2 %reshape.750 = bf16[2,2,24576]{2,1,0:T(2,128)(2,1)} reshape(bf16[1536,1,8,8]{3,2,1,0:T(8,128)(2,1)S(1)} %bitcast.300) | data formatting | bytes 393216
  109.2 4.1 %all-to-all-start.4 = ((bf16[2,2,24576]{2,1,0:T(2,128)(2,1)}), bf16[2,2,24576]{2,1,0:T(2,128)(2,1)}, u32[]{:S(2)}, u32[]{:S(2)}) async-start(bf16[2,2,24576]{2,1,0:T(2,128)(2,1)} %reshape.750), calls=%async_computation.4 | async-start | bytes 393216 | tf_op jit(solution)/shard_map/all_to_all | solution.py:121
  118.9 4.5 %reshape.745 = bf16[1536,1,8,8]{3,2,1,0:T(8,128)(2,1)S(1)} reshape(bf16[2,2,24576]{2,1,0:T(2,128)(2,1)} %all-to-all-done) | data formatting | bytes 393216
  123.5 2.4 copy.100
  127.7 4.5 %reshape.751 = bf16[1536,1,8,8]{3,2,1,0:T(8,128)(2,1)S(1)} reshape(bf16[2,2,24576]{2,1,0:T(2,128)(2,1)} %all-to-all-done.4) | data formatting | bytes 393216
  132.3 2.4 copy.112
  135.9 1.6 slice_dynamic-update-slice_fusion.5
  137.5 1.6 slice_dynamic-update-slice_fusion.4
  140.7 1.6 slice_dynamic-update-slice_fusion.2
  142.3 1.6 slice_dynamic-update-slice_fusion.1
  143.9 1.6 slice_dynamic-update-slice_fusion
  145.6 2.3 gather_fusion
  148.9 29.2 %while.14 = (s32[]{:T(128)}, bf16[6,128,128]{2,1,0:T(8,128)(2,1)S(1)}, f32[6,640,128]{2,1,0:T(8,128)}, f32[6,640,128]{2,1,0:T(8,128)}, bf16[6,128,128]{2,1,0:T(8...) while((s32[]{:T(128)}, ...), condition=%wide.region_6.8_spmd, body=%wide.region_5.7_spmd.sunk | while | flops 105529344 | bytes 2835589 | solution.py:189
  152.1 1.7 fusion.131
  156.9 1.7 fusion.131
  161.8 1.7 fusion.131
  166.7 1.7 fusion.131
  171.6 1.7 fusion.131
  176.4 1.7 fusion.131
  183.7 1.9 collective-permute-start.4
  189.0 2.6 %collective-permute-start.5 = (bf16[3,3,2,128,128]{4,3,2,1,0:T(8,128)(2,1)}, bf16[3,3,2,128,128]{4,3,2,1,0:T(8,128)(2,1)}, u32[]{:S(2)}, u32[]{:S(2)}) collective-permute-start(bf16[3,3,2,128,128]{4,3,2,1,0:T(8,128)(2,1)} %pad_maximum_fusion.9), channel_id=1, source_target_pairs={{0,2},{2,4},{4,6},{1,3},{3,5},{5,7},{8,10},{10,12},{12,14},{9,11},... | collective-permute-start | bytes 1769480 | tf_op jit(solution)/shard_map/ppermute | solution.py:24
  194.2 6.3 %collective-permute-done.5 = bf16[3,3,2,128,128]{4,3,2,1,0:T(8,128)(2,1)} collective-permute-done((bf16[3,3,2,128,128]{4,3,2,1,0:T(8,128)(2,1)}, bf16[3,3,2,128,128]{4,3,2,1,0:T(8,128)(2,1)}, u32[]{:S(2)}, u32[]{:S(2)}) %collective-permute-start.5) | collective-permute-done | bytes 589856 | tf_op jit(solution)/shard_map/ppermute | solution.py:24
  201.7 3.5 %collective-permute-start.7 = (bf16[3,3,2,128,128]{4,3,2,1,0:T(8,128)(2,1)S(1)}, bf16[3,3,2,128,128]{4,3,2,1,0:T(8,128)(2,1)S(1)}, u32[]{:S(2)}, u32[]{:S(2)}) collective-permute-start(bf16[3,3,2,128,128]{4,3,2,1,0:T(8,128)(2,1)S(1)} %pad_maximum_fusion.11), channel_id=1, source_target_pairs={{0,8},{8,16},{16,24},{1,9},{9,17},{17,25},{2,10},{10,18},{18,26},{... | collective-permute-start | bytes 1769480 | tf_op jit(solution)/shard_map/ppermute | solution.py:24
  207.6 3.4 %all-to-all-start.6 = ((bf16[2,8,8,768]{3,2,1,0:T(8,128)(2,1)}), bf16[2,8,8,768]{3,2,1,0:T(8,128)(2,1)S(1)}, u32[]{:S(2)}, u32[]{:S(2)}) async-start(bf16[2,8,8,768]{3,2,1,0:T(8,128)(2,1)} %reshape.550), calls=%async_computation.6 | async-start | bytes 393216 | tf_op jit(solution)/shard_map/all_to_all | solution.py:218
  212.5 4.6 %collective-permute-done.6 = bf16[3,3,2,128,128]{4,3,2,1,0:T(8,128)(2,1)} collective-permute-done((bf16[3,3,2,128,128]{4,3,2,1,0:T(8,128)(2,1)S(1)}, bf16[3,3,2,128,128]{4,3,2,1,0:T(8,128)(2,1)}, u32[]{:S(2)}, u32[]{:S(2)}) %collective-permute-start.6) | collective-permute-done | bytes 589856 | tf_op jit(solution)/shard_map/ppermute | solution.py:24
  222.1 3.4 %all-to-all-start.8 = ((bf16[2,8,8,768]{3,2,1,0:T(8,128)(2,1)}), bf16[2,8,8,768]{3,2,1,0:T(8,128)(2,1)S(1)}, u32[]{:S(2)}, u32[]{:S(2)}) async-start(bf16[2,8,8,768]{3,2,1,0:T(8,128)(2,1)} %reshape.552), calls=%async_computation.8 | async-start | bytes 393216 | tf_op jit(solution)/shard_map/all_to_all | solution.py:220
  226.6 3.7 %all-to-all-done.8 = bf16[2,8,8,768]{3,2,1,0:T(8,128)(2,1)S(1)} async-done(((bf16[2,8,8,768]{3,2,1,0:T(8,128)(2,1)}), bf16[2,8,8,768]{3,2,1,0:T(8,128)(2,1)S(1)}, u32[]{:S(2)}, u32[]{:S(2)}) %all-to-all-start.8) | async-done | bytes 196640 | tf_op jit(solution)/shard_map/all_to_all | solution.py:220
  230.3 3.4 %all-to-all-start.7 = ((bf16[2,8,8,768]{3,2,1,0:T(8,128)(2,1)}), bf16[2,8,8,768]{3,2,1,0:T(8,128)(2,1)S(1)}, u32[]{:S(2)}, u32[]{:S(2)}) async-start(bf16[2,8,8,768]{3,2,1,0:T(8,128)(2,1)} %reshape.551), calls=%async_computation.7 | async-start | bytes 393216 | tf_op jit(solution)/shard_map/all_to_all | solution.py:219
  235.1 3.4 %all-to-all-done.7 = bf16[2,8,8,768]{3,2,1,0:T(8,128)(2,1)S(1)} async-done(((bf16[2,8,8,768]{3,2,1,0:T(8,128)(2,1)}), bf16[2,8,8,768]{3,2,1,0:T(8,128)(2,1)S(1)}, u32[]{:S(2)}, u32[]{:S(2)}) %all-to-all-start.7) | async-done | bytes 196640 | tf_op jit(solution)/shard_map/all_to_all | solution.py:219
  (258 shorter events, 87.1 us)
Async XLA Ops:
  0.6 20.0 %copy-start.4 = (bf16[1,8,8,1536]{3,2,1,0:T(8,128)(2,1)S(1)}, bf16[1,8,8,1536]{3,2,1,0:T(8,128)(2,1)}, u32[]{:S(2)}) copy-start(bf16[1,8,8,1536]{3,2,1,0:T(8,128)(2,1)} %param.13) | copy-start | bytes 589828
  2.3 25.2 %all-to-all-start.2 = ((bf16[2,1,8,8,768]{4,3,2,1,0:T(8,128)(2,1)}), bf16[2,1,8,8,768]{4,3,2,1,0:T(8,128)(2,1)S(1)}, u32[]{:S(2)}, u32[]{:S(2)}) async-start(bf16[2,1,8,8,768]{4,3,2,1,0:T(8,128)(2,1)} %pad_maximum_fusion.13), calls=%async_computation.2 | async-start | bytes 393216 | tf_op jit(solution)/shard_map/all_to_all | solution.py:11
  8.0 6.2 %copy-start.15 = (s32[3]{0:T(128)}, s32[3]{0:T(128)S(1)}, u32[]{:S(2)}) copy-start(s32[3]{0:T(128)S(1)} %get-tuple-element.188) | copy-start | bytes 40
  8.0 10.5 %copy-start.16 = (s32[3]{0:T(128)}, s32[3]{0:T(128)S(1)}, u32[]{:S(2)}) copy-start(s32[3]{0:T(128)S(1)} %get-tuple-element.184) | copy-start | bytes 40
  8.0 10.5 %copy-start.17 = (s32[3]{0:T(128)}, s32[3]{0:T(128)S(1)}, u32[]{:S(2)}) copy-start(s32[3]{0:T(128)S(1)} %get-tuple-element.185) | copy-start | bytes 40
  8.0 10.5 %copy-start.18 = (s32[3]{0:T(128)}, s32[3]{0:T(128)S(1)}, u32[]{:S(2)}) copy-start(s32[3]{0:T(128)S(1)} %get-tuple-element.183) | copy-start | bytes 40
  8.0 10.5 %copy-start.19 = (s32[3]{0:T(128)}, s32[3]{0:T(128)S(1)}, u32[]{:S(2)}) copy-start(s32[3]{0:T(128)S(1)} %get-tuple-element.186) | copy-start | bytes 40
  8.0 10.5 %copy-start.21 = (s32[3]{0:T(128)}, s32[3]{0:T(128)S(1)}, u32[]{:S(2)}) copy-start(s32[3]{0:T(128)S(1)} %get-tuple-element.187) | copy-start | bytes 40
  22.8 4.1 %copy-start.32 = (s32[8,1]{0,1:T(1,128)S(1)}, s32[8,1]{0,1:T(1,128)}, u32[]{:S(2)}) copy-start(s32[8,1]{0,1:T(1,128)} %constant.90) | copy-start | bytes 100
  22.9 4.1 %copy-start.33 = (s32[8,1]{0,1:T(1,128)S(1)}, s32[8,1]{0,1:T(1,128)}, u32[]{:S(2)}) copy-start(s32[8,1]{0,1:T(1,128)} %constant.89) | copy-start | bytes 100
  22.9 4.1 %copy-start.35 = (s32[3]{0:T(128)S(1)}, s32[3]{0:T(128)}, u32[]{:S(2)}) copy-start(s32[3]{0:T(128)} %compare_select_fusion.8) | copy-start | bytes 40
  22.9 8.1 %copy-start.34 = (s32[3]{0:T(128)S(1)}, s32[3]{0:T(128)}, u32[]{:S(2)}) copy-start(s32[3]{0:T(128)} %compare_select_fusion.9) | copy-start | bytes 40
  27.6 8.2 %all-to-all-start.1 = ((bf16[2,2,24576]{2,1,0:T(2,128)(2,1)}), bf16[2,2,24576]{2,1,0:T(2,128)(2,1)S(1)}, u32[]{:S(2)}, u32[]{:S(2)}) async-start(bf16[2,2,24576]{2,1,0:T(2,128)(2,1)} %reshape.746), calls=%async_computation.1 | async-start | bytes 393216 | tf_op jit(solution)/shard_map/all_to_all | solution.py:119
  35.8 49.3 %all-to-all-start.3 = ((f32[2,1,384]{2,1,0:T(1,128)}), f32[2,1,384]{2,1,0:T(1,128)}, u32[]{:S(2)}, u32[]{:S(2)}) async-start(f32[2,1,384]{2,1,0:T(1,128)} %reshape.748), calls=%async_computation.3 | async-start | bytes 6144 | tf_op jit(solution)/shard_map/all_to_all | solution.py:124
  45.2 4.4 %copy-start.30 = (pred[3]{0:T(512)(128)(4,1)S(1)}, pred[3]{0:T(512)(128)(4,1)}, u32[]{:S(2)}) copy-start(pred[3]{0:T(512)(128)(4,1)} %compare_and_fusion.5) | copy-start | bytes 13
  45.3 4.4 %copy-start.29 = (pred[3]{0:T(512)(128)(4,1)S(1)}, pred[3]{0:T(512)(128)(4,1)}, u32[]{:S(2)}) copy-start(pred[3]{0:T(512)(128)(4,1)} %compare_and_fusion.7) | copy-start | bytes 13
  45.3 4.5 %copy-start.28 = (pred[3]{0:T(512)(128)(4,1)S(1)}, pred[3]{0:T(512)(128)(4,1)}, u32[]{:S(2)}) copy-start(pred[3]{0:T(512)(128)(4,1)} %compare_and_fusion.6) | copy-start | bytes 13
  48.1 5.5 %copy-start.27 = (pred[3]{0:T(512)(128)(4,1)S(1)}, pred[3]{0:T(512)(128)(4,1)}, u32[]{:S(2)}) copy-start(pred[3]{0:T(512)(128)(4,1)} %compare_and_fusion.1) | copy-start | bytes 13
  48.9 4.9 %copy-start.26 = (pred[3]{0:T(512)(128)(4,1)S(1)}, pred[3]{0:T(512)(128)(4,1)}, u32[]{:S(2)}) copy-start(pred[3]{0:T(512)(128)(4,1)} %compare_and_fusion.2) | copy-start | bytes 13
  49.6 4.3 %copy-start.25 = (pred[3]{0:T(512)(128)(4,1)S(1)}, pred[3]{0:T(512)(128)(4,1)}, u32[]{:S(2)}) copy-start(pred[3]{0:T(512)(128)(4,1)} %compare_and_fusion.3) | copy-start | bytes 13
  49.9 5.5 %copy-start = (bf16[1,8,8,1536]{3,2,1,0:T(8,128)(2,1)S(1)}, bf16[1,8,8,1536]{3,2,1,0:T(8,128)(2,1)}, u32[]{:S(2)}) copy-start(bf16[1,8,8,1536]{3,2,1,0:T(8,128)(2,1)} %param.16) | copy-start | bytes 589828
  49.9 5.5 %copy-start.5 = (bf16[1,8,8,1536]{3,2,1,0:T(8,128)(2,1)S(1)}, bf16[1,8,8,1536]{3,2,1,0:T(8,128)(2,1)}, u32[]{:S(2)}) copy-start(bf16[1,8,8,1536]{3,2,1,0:T(8,128)(2,1)} %param.15) | copy-start | bytes 589828
  50.0 7.0 %copy-start.24 = (pred[3]{0:T(512)(128)(4,1)S(1)}, pred[3]{0:T(512)(128)(4,1)}, u32[]{:S(2)}) copy-start(pred[3]{0:T(512)(128)(4,1)} %compare_and_fusion.4) | copy-start | bytes 13
  50.0 15.0 %collective-permute-start = (bf16[3,3,2,128,128]{4,3,2,1,0:T(8,128)(2,1)S(1)}, bf16[3,3,2,128,128]{4,3,2,1,0:T(8,128)(2,1)S(1)}, u32[]{:S(2)}, u32[]{:S(2)}) collective-permute-start(bf16[3,3,2,128,128]{4,3,2,1,0:T(8,128)(2,1)S(1)} %pad_maximum_fusion.4), channel_id=1, source_target_pairs={{0,8},{8,16},{16,24},{1,9},{9,17},{17,25},{2,10},{10,18},{18,26},{... | collective-permute-start | bytes 1769480 | tf_op jit(solution)/shard_map/ppermute | solution.py:24
  54.1 15.5 %collective-permute-start.1 = (bf16[3,3,2,128,128]{4,3,2,1,0:T(8,128)(2,1)S(1)}, bf16[3,3,2,128,128]{4,3,2,1,0:T(8,128)(2,1)S(1)}, u32[]{:S(2)}, u32[]{:S(2)}) collective-permute-start(bf16[3,3,2,128,128]{4,3,2,1,0:T(8,128)(2,1)S(1)} %pad_maximum_fusion.5), channel_id=1, source_target_pairs={{8,0},{16,8},{24,16},{9,1},{17,9},{25,17},{10,2},{18,10},{26,18},{... | collective-permute-start | bytes 1769480 | tf_op jit(solution)/shard_map/ppermute | solution.py:24
  56.2 15.5 %copy-start.14 = (s32[24]{0:T(128)S(1)}, s32[24]{0:T(128)}, u32[]{:S(2)}) copy-start(s32[24]{0:T(128)} %reshape.627) | copy-start | bytes 292
  69.6 2.8 %copy-start.1 = (bf16[3,3,2,128,128]{4,3,2,1,0:T(8,128)(2,1)}, bf16[3,3,2,128,128]{4,3,2,1,0:T(8,128)(2,1)S(1)}, u32[]{:S(2)}) copy-start(bf16[3,3,2,128,128]{4,3,2,1,0:T(8,128)(2,1)S(1)} %collective-permute-done.1) | copy-start | bytes 1769476
  69.7 11.2 %collective-permute-start.2 = (bf16[3,3,2,128,128]{4,3,2,1,0:T(8,128)(2,1)S(1)}, bf16[3,3,2,128,128]{4,3,2,1,0:T(8,128)(2,1)S(1)}, u32[]{:S(2)}, u32[]{:S(2)}) collective-permute-start(bf16[3,3,2,128,128]{4,3,2,1,0:T(8,128)(2,1)S(1)} %pad_maximum_fusion.6), channel_id=1, source_target_pairs={{0,2},{2,4},{4,6},{1,3},{3,5},{5,7},{8,10},{10,12},{12,14},{9,11},... | collective-permute-start | bytes 1769480 | tf_op jit(solution)/shard_map/ppermute | solution.py:24
  71.7 2.2 copy-start.23
  73.2 15.1 %copy-start.20 = (s32[3]{0:T(128)S(1)}, s32[3]{0:T(128)}, u32[]{:S(2)}) copy-start(s32[3]{0:T(128)} %get-tuple-element.130) | copy-start | bytes 40
  73.2 15.1 %copy-start.22 = (s32[3]{0:T(128)S(1)}, s32[3]{0:T(128)}, u32[]{:S(2)}) copy-start(s32[3]{0:T(128)} %copy-done.21) | copy-start | bytes 40
  80.9 7.5 %copy-start.2 = (bf16[3,3,2,128,128]{4,3,2,1,0:T(8,128)(2,1)}, bf16[3,3,2,128,128]{4,3,2,1,0:T(8,128)(2,1)S(1)}, u32[]{:S(2)}) copy-start(bf16[3,3,2,128,128]{4,3,2,1,0:T(8,128)(2,1)S(1)} %collective-permute-done.2) | copy-start | bytes 1769476
  83.2 52.7 %collective-permute-start.3 = (bf16[3,3,2,128,128]{4,3,2,1,0:T(8,128)(2,1)}, bf16[3,3,2,128,128]{4,3,2,1,0:T(8,128)(2,1)}, u32[]{:S(2)}, u32[]{:S(2)}) collective-permute-start(bf16[3,3,2,128,128]{4,3,2,1,0:T(8,128)(2,1)} %pad_maximum_fusion.7), channel_id=1, source_target_pairs={{2,0},{4,2},{6,4},{3,1},{5,3},{7,5},{10,8},{12,10},{14,12},{11,9},... | collective-permute-start | bytes 1769480 | tf_op jit(solution)/shard_map/ppermute | solution.py:24
  85.1 11.2 %all-to-all-start.5 = ((f32[2,1,384]{2,1,0:T(1,128)}), f32[2,1,384]{2,1,0:T(1,128)S(1)}, u32[]{:S(2)}, u32[]{:S(2)}) async-start(f32[2,1,384]{2,1,0:T(1,128)} %reshape.752), calls=%async_computation.5 | async-start | bytes 6144 | tf_op jit(solution)/shard_map/all_to_all | solution.py:125
  96.3 8.7 %copy-start.7 = (f32[2,1,384]{2,1,0:T(1,128)}, f32[2,1,384]{2,1,0:T(1,128)S(1)}, u32[]{:S(2)}) copy-start(f32[2,1,384]{2,1,0:T(1,128)S(1)} %all-to-all-done.5) | copy-start | bytes 9220
  96.3 12.9 %all-to-all-start = ((bf16[2,2,24576]{2,1,0:T(2,128)(2,1)}), bf16[2,2,24576]{2,1,0:T(2,128)(2,1)}, u32[]{:S(2)}, u32[]{:S(2)}) async-start(bf16[2,2,24576]{2,1,0:T(2,128)(2,1)} %reshape.744), calls=%async_computation | async-start | bytes 393216 | tf_op jit(solution)/shard_map/all_to_all | solution.py:118
  105.0 9.6 %copy-start.13 = (s32[6,4,1]{0,1,2:T(4,128)S(1)}, s32[6,4,1]{0,1,2:T(4,128)}, u32[]{:S(2)}) copy-start(s32[6,4,1]{0,1,2:T(4,128)} %fusion.43) | copy-start | bytes 292
  109.2 18.5 %all-to-all-start.4 = ((bf16[2,2,24576]{2,1,0:T(2,128)(2,1)}), bf16[2,2,24576]{2,1,0:T(2,128)(2,1)}, u32[]{:S(2)}, u32[]{:S(2)}) async-start(bf16[2,2,24576]{2,1,0:T(2,128)(2,1)} %reshape.750), calls=%async_computation.4 | async-start | bytes 393216 | tf_op jit(solution)/shard_map/all_to_all | solution.py:121
  181.8 4.5 %copy-start.8 = (s32[3]{0:T(128)S(1)}, s32[3]{0:T(128)}, u32[]{:S(2)}) copy-start(s32[3]{0:T(128)} %fusion.86) | copy-start | bytes 40
  181.8 5.1 %copy-start.9 = (s32[3]{0:T(128)S(1)}, s32[3]{0:T(128)}, u32[]{:S(2)}) copy-start(s32[3]{0:T(128)} %fusion.87) | copy-start | bytes 40
  183.7 10.4 %collective-permute-start.4 = (bf16[3,3,2,128,128]{4,3,2,1,0:T(8,128)(2,1)S(1)}, bf16[3,3,2,128,128]{4,3,2,1,0:T(8,128)(2,1)S(1)}, u32[]{:S(2)}, u32[]{:S(2)}) collective-permute-start(bf16[3,3,2,128,128]{4,3,2,1,0:T(8,128)(2,1)S(1)} %pad_maximum_fusion.8), channel_id=1, source_target_pairs={{2,0},{4,2},{6,4},{3,1},{5,3},{7,5},{10,8},{12,10},{14,12},{11,9},... | collective-permute-start | bytes 1769480 | tf_op jit(solution)/shard_map/ppermute | solution.py:24
  189.0 11.5 %collective-permute-start.5 = (bf16[3,3,2,128,128]{4,3,2,1,0:T(8,128)(2,1)}, bf16[3,3,2,128,128]{4,3,2,1,0:T(8,128)(2,1)}, u32[]{:S(2)}, u32[]{:S(2)}) collective-permute-start(bf16[3,3,2,128,128]{4,3,2,1,0:T(8,128)(2,1)} %pad_maximum_fusion.9), channel_id=1, source_target_pairs={{0,2},{2,4},{4,6},{1,3},{3,5},{5,7},{8,10},{10,12},{12,14},{9,11},... | collective-permute-start | bytes 1769480 | tf_op jit(solution)/shard_map/ppermute | solution.py:24
  201.7 10.8 %collective-permute-start.7 = (bf16[3,3,2,128,128]{4,3,2,1,0:T(8,128)(2,1)S(1)}, bf16[3,3,2,128,128]{4,3,2,1,0:T(8,128)(2,1)S(1)}, u32[]{:S(2)}, u32[]{:S(2)}) collective-permute-start(bf16[3,3,2,128,128]{4,3,2,1,0:T(8,128)(2,1)S(1)} %pad_maximum_fusion.11), channel_id=1, source_target_pairs={{0,8},{8,16},{16,24},{1,9},{9,17},{17,25},{2,10},{10,18},{18,26},{... | collective-permute-start | bytes 1769480 | tf_op jit(solution)/shard_map/ppermute | solution.py:24
  205.3 11.9 %collective-permute-start.6 = (bf16[3,3,2,128,128]{4,3,2,1,0:T(8,128)(2,1)S(1)}, bf16[3,3,2,128,128]{4,3,2,1,0:T(8,128)(2,1)}, u32[]{:S(2)}, u32[]{:S(2)}) collective-permute-start(bf16[3,3,2,128,128]{4,3,2,1,0:T(8,128)(2,1)S(1)} %pad_maximum_fusion.10), channel_id=1, source_target_pairs={{8,0},{16,8},{24,16},{9,1},{17,9},{25,17},{10,2},{18,10},{26,18},{... | collective-permute-start | bytes 1769480 | tf_op jit(solution)/shard_map/ppermute | solution.py:24
  207.6 14.4 %all-to-all-start.6 = ((bf16[2,8,8,768]{3,2,1,0:T(8,128)(2,1)}), bf16[2,8,8,768]{3,2,1,0:T(8,128)(2,1)S(1)}, u32[]{:S(2)}, u32[]{:S(2)}) async-start(bf16[2,8,8,768]{3,2,1,0:T(8,128)(2,1)} %reshape.550), calls=%async_computation.6 | async-start | bytes 393216 | tf_op jit(solution)/shard_map/all_to_all | solution.py:218
  212.5 4.6 %copy-start.3 = (bf16[3,3,2,128,128]{4,3,2,1,0:T(8,128)(2,1)}, bf16[3,3,2,128,128]{4,3,2,1,0:T(8,128)(2,1)S(1)}, u32[]{:S(2)}) copy-start(bf16[3,3,2,128,128]{4,3,2,1,0:T(8,128)(2,1)S(1)} %collective-permute-done.7) | copy-start | bytes 1769476
  222.1 8.2 %all-to-all-start.8 = ((bf16[2,8,8,768]{3,2,1,0:T(8,128)(2,1)}), bf16[2,8,8,768]{3,2,1,0:T(8,128)(2,1)S(1)}, u32[]{:S(2)}, u32[]{:S(2)}) async-start(bf16[2,8,8,768]{3,2,1,0:T(8,128)(2,1)} %reshape.552), calls=%async_computation.8 | async-start | bytes 393216 | tf_op jit(solution)/shard_map/all_to_all | solution.py:220
  230.3 8.2 %all-to-all-start.7 = ((bf16[2,8,8,768]{3,2,1,0:T(8,128)(2,1)}), bf16[2,8,8,768]{3,2,1,0:T(8,128)(2,1)S(1)}, u32[]{:S(2)}, u32[]{:S(2)}) async-start(bf16[2,8,8,768]{3,2,1,0:T(8,128)(2,1)} %reshape.551), calls=%async_computation.7 | async-start | bytes 393216 | tf_op jit(solution)/shard_map/all_to_all | solution.py:219
  (5 other events, 5.9 us)
